TPU v7x, 32 devices: a whole 2x2x4 slice. The times are simulated.
32 devices in a mesh: dp: 4 (over y, core), row: 4 (over z), col: 2 (over x).
Axes of the slice: x: 2, y: 2, z: 4, core: 2. Of those that a mesh axis runs over, the one named last changes fastest.
Arguments:
- tokens: bfloat16 [4096, 6144], P(('dp', 'col'), 'row'), may hold values from -6 to 6
- weight_in: bfloat16 [6144, 12288], P('row', 'col'), may hold values from -0.078125 to 0.078125
- weight_out: bfloat16 [12288, 6144], P('col', 'row'), may hold values from -0.0546875 to 0.0546875
- cotangent: bfloat16 [4096, 6144], P(('dp', 'col'), 'row'), may hold values from -1.5 to 1.5
Outputs:
- input_grad: bfloat16 [4096, 6144], P(('dp', 'col'), 'row')
- weight_in_grad: bfloat16 [6144, 12288], P('row', ('col', 'dp'))
- weight_out_grad: bfloat16 [12288, 6144], P(('col', 'dp'), 'row')
All inputs are finite; a program needn't handle non-finite values.
Results may differ from a plain program's by a relative error of at most 0.0051.
Values may be sent and summed in bfloat16 or wider, within the bound.
A program may use at most 320 MiB of HBM per device.

v0:
```python
import math

import jax
import jax.numpy as jnp
from jax import lax
from jax.sharding import PartitionSpec as P


def gelu_exact(values):
    return 0.5 * values * (1.0 + jax.scipy.special.erf(values / math.sqrt(2.0)))


def gelu_slope(values):
    cumulative = 0.5 * (1.0 + jax.scipy.special.erf(values / math.sqrt(2.0)))
    density = jnp.exp(-0.5 * values * values) / math.sqrt(2.0 * math.pi)
    return cumulative + values * density


def contract_last(left, right):
    return lax.dot_general(
        left, right, (((1,), (1,)), ((), ())), preferred_element_type=jnp.float32
    )


def contract_first(left, right):
    return lax.dot_general(
        left, right, (((0,), (0,)), ((), ())), preferred_element_type=jnp.float32
    )


def shards(tokens, weight_in, weight_out, cotangent):
    tok_all, cot_all = (
        lax.all_gather(tokens, "col", axis=0, tiled=True),
        lax.all_gather(cotangent, "col", axis=0, tiled=True),
    )
    hidden_cols = weight_in.shape[1]
    forward = jnp.dot(tok_all, weight_in, preferred_element_type=jnp.float32)
    backward = contract_last(cot_all, weight_out)
    summed = lax.psum_scatter(
        jnp.concatenate([forward, backward], axis=1), "row", scatter_dimension=0, tiled=True
    )
    preact = summed[:, :hidden_cols]
    grad_hidden = summed[:, hidden_cols:]
    activated = gelu_exact(preact).astype(jnp.bfloat16)
    grad_preact = (grad_hidden * gelu_slope(preact)).astype(jnp.bfloat16)
    acted_all, grad_all = (
        lax.all_gather(activated, "row", axis=0, tiled=True),
        lax.all_gather(grad_preact, "row", axis=0, tiled=True),
    )
    in_partial = contract_first(tok_all, grad_all)
    out_partial = contract_first(acted_all, cot_all)
    input_grad = lax.psum_scatter(
        contract_last(grad_all, weight_in), "col", scatter_dimension=0, tiled=True
    )
    in_total, out_total = (
        lax.psum_scatter(in_partial, "dp", scatter_dimension=1, tiled=True),
        lax.psum_scatter(out_partial, "dp", scatter_dimension=0, tiled=True),
    )
    return (
        input_grad.astype(jnp.bfloat16),
        in_total.astype(jnp.bfloat16),
        out_total.astype(jnp.bfloat16),
    )


def solution(mesh):
    return jax.shard_map(
        shards,
        mesh=mesh,
        in_specs=(
            P(("dp", "col"), "row"),
            P("row", "col"),
            P("col", "row"),
            P(("dp", "col"), "row"),
        ),
        out_specs=(P(("dp", "col"), "row"), P("row", ("col", "dp")), P(("col", "dp"), "row")),
        check_vma=False,
    )
```

profile of v0, /device:TPU:0, one launch (start us, length us, event | category | flops | bytes accessed | tf_op | source)
XLA Modules:
  0.0 2052.6 jit_solution(10461041267749841482)
XLA Ops:
  7.2 0.0 all-gather.7.cloned.1.call-start
  7.2 0.7 all-gather.7.cloned.1.call-update
  7.9 0.0 all-gather.5.cloned.1.call-start
  7.9 0.7 all-gather.5.cloned.1.call-update
  8.6 0.0 reduce-scatter.5.cloned.1.call-start
  8.7 48.5 %all-gather.7.cloned.1.call-done = bf16[1024,1536]{1,0:T(8,128)(2,1)} async-done(((bf16[512,1536]{1,0:T(8,128)(2,1)}), bf16[1024,1536]{1,0:T(8,128)(2,1)}) %all-gather.7.cloned.1.call-update) | async-done | bytes 3145744 | tf_op jit(solution)/shard_map/all_gather | solution.py:34
  57.2 26.4 %fusion.7 = f32[1024,6144]{1,0:T(8,128)} fusion(bf16[1024,1536]{1,0:T(8,128)(2,1)} %all-gather.7.cloned.1.call-done, bf16[6144,1536]{1,0:T(8,128)(2,1)} %param.6), kind=kOutput, calls=%fused_computation.12 | convolution fusion | flops 19327352832 | bytes 47185920 | tf_op jit(solution)/shard_map/dot_general | solution.py:20
  83.6 20.1 all-gather.5.cloned.1.call-done
  103.7 26.2 %fusion.6 = f32[1024,6144]{1,0:T(8,128)} fusion(bf16[1024,1536]{1,0:T(8,128)(2,1)} %all-gather.5.cloned.1.call-done, bf16[1536,6144]{1,0:T(8,128)(2,1)} %param.5), kind=kOutput, calls=%fused_computation.11 | convolution fusion | flops 19327352832 | bytes 47185920 | tf_op jit(solution)/shard_map/dot_general | solution.py:37
  129.9 34.2 %pad_maximum_fusion = f32[1024,12288]{1,0:T(8,128)} fusion(f32[1024,6144]{1,0:T(8,128)} %fusion.7, f32[1024,6144]{1,0:T(8,128)} %fusion.6), kind=kLoop, calls=%fused_computation | loop fusion | flops 12582912 | bytes 100663296 | tf_op jit(solution)/shard_map/concatenate | solution.py:40
  164.1 0.0 reduce-scatter.5.cloned.1.call-update
  164.1 0.0 all-gather.9.cloned.1.call-start
  164.2 820.8 %reduce-scatter.5.cloned.1.call-done = f32[256,12288]{1,0:T(8,128)} async-done(((f32[1024,12288]{1,0:T(8,128)}), f32[256,12288]{1,0:T(8,128)}) %reduce-scatter.5.cloned.1.call-update) | async-done | bytes 12582928 | tf_op jit(solution)/shard_map/reduce_scatter | solution.py:39
  984.9 9.4 multiply_convert_fusion
  994.4 0.0 all-gather.11.cloned.1.call-start
  994.4 0.5 all-gather.11.cloned.1.call-update
  994.9 0.0 reduce-scatter.7.cloned.1.call-start
  995.0 219.8 %all-gather.9.cloned.1.call-done = bf16[1024,6144]{1,0:T(8,128)(2,1)} async-done(((bf16[256,6144]{1,0:T(8,128)(2,1)}), bf16[1024,6144]{1,0:T(8,128)(2,1)}) %all-gather.9.cloned.1.call-update) | async-done | bytes 12582928 | tf_op jit(solution)/shard_map/all_gather | solution.py:48
  1214.8 26.3 %fusion.8 = f32[1024,1536]{1,0:T(8,128)} fusion(bf16[1024,6144]{1,0:T(8,128)(2,1)} %all-gather.9.cloned.1.call-done, bf16[1536,6144]{1,0:T(8,128)(2,1)} %param.5), kind=kOutput, calls=%fused_computation.13 | convolution fusion | flops 19327352832 | bytes 37748736 | tf_op jit(solution)/shard_map/dot_general | solution.py:20
  1241.1 0.2 reduce-scatter.9.cloned.1.call-start
  1241.4 1.7 copy-done.1
  1243.0 27.1 %convolution_bitcast_fusion = f32[1536,6144]{0,1:T(8,128)} fusion(bf16[1024,6144]{1,0:T(8,128)(2,1)} %all-gather.9.cloned.1.call-done, bf16[1024,1536]{1,0:T(8,128)(2,1)S(1)} %copy-done.1), kind=kOutput, calls=%fused_computation.1 | convolution fusion | flops 19327352832 | bytes 53477376 | tf_op jit(solution)/shard_map/dot_general | solution.py:26
  1270.1 0.3 reduce-scatter.11.cloned.1.call-start
  1270.4 162.9 %all-gather.11.cloned.1.call-done = bf16[1024,6144]{1,0:T(8,128)(2,1)} async-done(((bf16[256,6144]{1,0:T(8,128)(2,1)}), bf16[1024,6144]{1,0:T(8,128)(2,1)}) %all-gather.11.cloned.1.call-update) | async-done | bytes 12582928 | tf_op jit(solution)/shard_map/all_gather | solution.py:47
  1433.3 26.9 %fusion.9 = f32[6144,1536]{1,0:T(8,128)} fusion(bf16[1024,6144]{1,0:T(8,128)(2,1)} %all-gather.11.cloned.1.call-done, bf16[1024,1536]{1,0:T(8,128)(2,1)S(1)} %copy-done), kind=kOutput, calls=%fused_computation.14 | convolution fusion | flops 19327352832 | bytes 53477376 | tf_op jit(solution)/shard_map/dot_general | solution.py:26
  1460.2 50.6 %reduce-scatter.7.cloned.1.call-done = f32[512,1536]{1,0:T(8,128)} async-done(((f32[1024,1536]{1,0:T(8,128)}), f32[512,1536]{1,0:T(8,128)}) %reduce-scatter.7.cloned.1.call-update) | async-done | bytes 3145744 | tf_op jit(solution)/shard_map/reduce_scatter | solution.py:52
  1510.8 3.2 convert_element_type.16
  1514.0 261.0 %reduce-scatter.9.cloned.1.call-done = f32[1536,1536]{0,1:T(8,128)} async-done(((f32[1536,6144]{0,1:T(8,128)}), f32[1536,1536]{0,1:T(8,128)}) %reduce-scatter.9.cloned.1.call-update) | async-done | bytes 9437200 | tf_op jit(solution)/shard_map/reduce_scatter | solution.py:56
  1775.0 6.4 convert_element_type.17
  1781.4 6.9 copy.7
  1788.4 250.9 %reduce-scatter.11.cloned.1.call-done = f32[1536,1536]{1,0:T(8,128)} async-done(((f32[6144,1536]{1,0:T(8,128)}), f32[1536,1536]{1,0:T(8,128)}) %reduce-scatter.11.cloned.1.call-update) | async-done | bytes 9437200 | tf_op jit(solution)/shard_map/reduce_scatter | solution.py:57
  2039.3 6.4 convert_element_type.19
  (7 shorter events, 0.1 us)
Async XLA Ops:
  7.2 50.0 %all-gather.7.cloned.1.call-start = ((), (), s32[]{:S(2)}) async-start(), calls=%async_computation.5 | async-start | bytes 4718592 | tf_op jit(solution)/shard_map/all_gather | solution.py:34
  7.9 95.8 %all-gather.5.cloned.1.call-start = ((), (), s32[]{:S(2)}) async-start(), calls=%async_computation.4 | async-start | bytes 4718592 | tf_op jit(solution)/shard_map/all_gather | solution.py:33
  8.6 976.3 %reduce-scatter.5.cloned.1.call-start = ((), (), s32[]{:S(2)}) async-start(), calls=%async_computation.6 | async-start | bytes 62914560 | tf_op jit(solution)/shard_map/reduce_scatter | solution.py:39
  164.1 1050.7 %all-gather.9.cloned.1.call-start = ((), (), s32[]{:S(2)}) async-start(), calls=%async_computation.7 | async-start | bytes 15728640 | tf_op jit(solution)/shard_map/all_gather | solution.py:48
  994.4 438.9 %all-gather.11.cloned.1.call-start = ((), (), s32[]{:S(2)}) async-start(), calls=%async_computation.10 | async-start | bytes 15728640 | tf_op jit(solution)/shard_map/all_gather | solution.py:47
  994.9 515.9 %reduce-scatter.7.cloned.1.call-start = ((), (), s32[]{:S(2)}) async-start(), calls=%async_computation.8 | async-start | bytes 9437184 | tf_op jit(solution)/shard_map/reduce_scatter | solution.py:52
  1241.1 1.9 copy-start.1
  1241.1 533.9 %reduce-scatter.9.cloned.1.call-start = ((), (), s32[]{:S(2)}) async-start(), calls=%async_computation.9 | async-start | bytes 47185920 | tf_op jit(solution)/shard_map/reduce_scatter | solution.py:56
  1270.1 163.2 %copy-start = (bf16[1024,1536]{1,0:T(8,128)(2,1)S(1)}, bf16[1024,1536]{1,0:T(8,128)(2,1)}, u32[]{:S(2)}) copy-start(bf16[1024,1536]{1,0:T(8,128)(2,1)} %all-gather.7.cloned.1.call-done) | copy-start | bytes 9437188
  1270.1 769.2 %reduce-scatter.11.cloned.1.call-start = ((), (), s32[]{:S(2)}) async-start(), calls=%async_computation.11 | async-start | bytes 47185920 | tf_op jit(solution)/shard_map/reduce_scatter | solution.py:57
Sparse Core Ops, SparseCore 0:
  9.5 47.6 all-gather.6
  58.7 44.9 all-gather.4
  164.2 820.6 reduce-scatter.4
  994.5 220.2 all-gather.8
  1216.8 216.3 all-gather.10
  1435.5 75.2 reduce-scatter.6
  1513.4 261.5 reduce-scatter.8
  1777.8 261.5 reduce-scatter.10
where the time goes:
time: 2050 us
  waiting for transfers between devices  1840 us (90%)
  matrix products  133 us (6%)
  other arithmetic  59.7 us (3%)
    reduce_scatter x1, waiting for transfers between devices, shards(): lax.psum_scatter(jnp.concatenate([forward, backward], axis=1), 'row', sca...  821 us
    reduce_scatter x1, waiting for transfers between devices, shards(): lax.psum_scatter(in_partial, 'dp', scatter_dimension=1, tiled=True)  261 us
    reduce_scatter x1, waiting for transfers between devices, shards(): lax.psum_scatter(out_partial, 'dp', scatter_dimension=0, tiled=True)  251 us
    all_gather x1, waiting for transfers between devices, shards(): lax.all_gather(grad_preact, 'row', axis=0, tiled=True)  220 us
    all_gather x1, waiting for transfers between devices, shards(): lax.all_gather(activated, 'row', axis=0, tiled=True)  163 us
    dot_general x2, matrix products, contract_first(): lax.dot_general(left, right, (((0,), (0,)), ((), ())), preferred_element_...  54 us
    dot_general x2, matrix products, contract_last(): lax.dot_general(left, right, (((1,), (1,)), ((), ())), preferred_element_...  52.7 us
    reduce_scatter x1, waiting for transfers between devices, shards(): lax.psum_scatter(contract_last(grad_all, weight_in), 'col', scatter_dimen...  50.6 us
  transfers between devices with their start and end apart: 8, of which 8 were waited for; matrix products, arithmetic and copies ran while one was open for 6% of the time, Pallas kernels for 0%

commit v1 on v0

v1 whole, which is shorter than its diff:
```python
import math

import jax
import jax.numpy as jnp
from jax import lax
from jax.sharding import PartitionSpec as P


def gelu_exact(values):
    return 0.5 * values * (1.0 + jax.scipy.special.erf(values / math.sqrt(2.0)))


def gelu_slope(values):
    cumulative = 0.5 * (1.0 + jax.scipy.special.erf(values / math.sqrt(2.0)))
    density = jnp.exp(-0.5 * values * values) / math.sqrt(2.0 * math.pi)
    return cumulative + values * density


def contract_last(left, right):
    return lax.dot_general(
        left, right, (((1,), (1,)), ((), ())), preferred_element_type=jnp.float32
    )


def contract_first(left, right):
    return lax.dot_general(
        left, right, (((0,), (0,)), ((), ())), preferred_element_type=jnp.float32
    )


def wide(value):
    return value.astype(jnp.float32)


def narrow(value):
    return value.astype(jnp.bfloat16)


def shards(n_dp, n_row, n_col, tokens, weight_in, weight_out, cotangent):
    rows = tokens.shape[0]
    hidden = weight_in.shape[1]
    part = hidden // n_dp
    width = 256 if part % 256 == 0 else 128
    dp = lax.axis_index("dp")

    def gather(block):
        blocks = [block]
        for shift in range(1, n_col):
            pairs = [(i, (i - shift) % n_col) for i in range(n_col)]
            blocks.append(lax.ppermute(block, "col", pairs))
        return jnp.concatenate(blocks, axis=0)

    tok_all, cot_all = gather(tokens), gather(cotangent)

    slots, bits = [0], []
    bit = n_dp // 2
    while bit:
        slots = slots + [s ^ bit for s in slots]
        bits.insert(0, bit)
        bit //= 2

    row = lax.axis_index("row")

    class Line:
        def __init__(self, units):
            self.units, self.own, self.right, self.left = units, {}, {}, {}
            self.steps = units + n_row - 2

        def pick(self, held, first, sign):
            cases = [held.get(first + sign * z) for z in range(n_row)]
            some = next(c for c in cases if c is not None)
            return wide(lax.select_n(row, *[some if c is None else c for c in cases]))

        def step(self, t):
            right = self.pick(self.own, t, -1)
            left = self.pick(self.own, t - (n_row - 1), 1)
            if t:
                right = right + wide(self.right[t - 1])
                left = left + wide(self.left[t - 1])
            up = [(z, z + 1) for z in range(n_row - 1)]
            down = [(z + 1, z) for z in range(n_row - 1)]
            self.right[t] = lax.ppermute(narrow(right), "row", up)
            self.left[t] = lax.ppermute(narrow(left), "row", down)

        def total(self, c):
            right = self.pick({k: v for k, v in self.right.items() if k >= c}, c - 1, 1)
            left = self.pick({k: v for k, v in self.left.items() if k >= c}, c + n_row - 2, -1)
            zero = jnp.zeros((), jnp.float32)
            return (
                self.own[c]
                + jnp.where(row > 0, right, zero)
                + jnp.where(row < n_row - 1, left, zero)
            )

    def exchange(keep, send, bit):
        pairs = [(i, i ^ bit) for i in range(n_dp)]
        return keep + wide(lax.ppermute(narrow(send), "dp", pairs))

    def replica_sum(total, axis):
        for bit in bits:
            half = total.shape[axis] // 2
            keep = lax.slice_in_dim(total, 0, half, axis=axis)
            send = lax.slice_in_dim(total, half, 2 * half, axis=axis)
            total = exchange(keep, send, bit)
        return narrow(total)

    starts = list(range(0, part, width))
    halves = 2
    units = len(starts) * halves
    half = tok_all.shape[0] // halves
    forward, backward = Line(units), Line(units)
    acts, slopes = {}, {}
    in_grads, out_grads, input_total = [], [], None
    weights = {}

    def load(k):
        places = [(dp ^ s) * part + starts[k] for s in slots]
        weights[k] = (
            jnp.concatenate(
                [lax.dynamic_slice_in_dim(weight_in, p, width, axis=1) for p in places], axis=1
            ),
            jnp.concatenate(
                [lax.dynamic_slice_in_dim(weight_out, p, width, axis=0) for p in places], axis=0
            ),
        )

    def block(array, h):
        return array[h * half : (h + 1) * half]

    def ready_forward(c):
        if c < units:
            if c // halves not in weights:
                load(c // halves)
            rows_in = block(tok_all, c % halves)
            forward.own[c] = jnp.dot(
                rows_in, weights[c // halves][0], preferred_element_type=jnp.float32
            )

    def ready_backward(c):
        if c < units:
            backward.own[c] = contract_last(block(cot_all, c % halves), weights[c // halves][1])

    def fence(line, t, work):
        if t:
            line.right[t - 1], line.left[t - 1], work = lax.optimization_barrier(
                (line.right[t - 1], line.left[t - 1], work)
            )
        return work

    ready_forward(0)
    ready_backward(0)
    for t in range(forward.steps + 1):
        c = t - (n_row - 1)
        fresh = forward.own.get(t)
        fresh = fence(forward, t, fresh)
        if fresh is not None:
            forward.own[t] = fresh
        if t < forward.steps:
            forward.step(t)
        ready_forward(t + 1)
        fresh = backward.own.get(t)
        fresh = fence(backward, t, (fresh, forward.own.get(t + 1)))
        if fresh[0] is not None:
            backward.own[t] = fresh[0]
        if fresh[1] is not None:
            forward.own[t + 1] = fresh[1]
        if t < backward.steps:
            backward.step(t)
        ready_backward(t + 1)
        if c < 0:
            continue
        preact, grad_hidden = forward.total(c), backward.total(c)
        acts[c] = narrow(gelu_exact(preact))
        slopes[c] = narrow(grad_hidden * gelu_slope(preact))
        if c % halves == halves - 1:
            k = c // halves
            mine = range(k * halves, (k + 1) * halves)
            activated = jnp.concatenate([acts[i] for i in mine], axis=0)
            grad_preact = jnp.concatenate([slopes[i] for i in mine], axis=0)
            in_grads.append(replica_sum(contract_first(tok_all, grad_preact), 1))
            out_grads.append(replica_sum(contract_first(activated, cot_all), 0))
            term = contract_last(grad_preact, weights[k][0])
            input_total = term if input_total is None else input_total + term

    input_grad = input_total[:rows]
    for shift in range(1, n_col):
        pairs = [(i, (i + shift) % n_col) for i in range(n_col)]
        piece = narrow(input_total[shift * rows : (shift + 1) * rows])
        input_grad = input_grad + wide(lax.ppermute(piece, "col", pairs))
    return (
        narrow(input_grad),
        jnp.concatenate(in_grads, axis=1),
        jnp.concatenate(out_grads, axis=0),
    )


def solution(mesh):
    sizes = [mesh.shape[name] for name in ("dp", "row", "col")]

    def body(*arrays):
        return shards(*sizes, *arrays)

    return jax.shard_map(
        body,
        mesh=mesh,
        in_specs=(
            P(("dp", "col"), "row"),
            P("row", "col"),
            P("col", "row"),
            P(("dp", "col"), "row"),
        ),
        out_specs=(P(("dp", "col"), "row"), P("row", ("col", "dp")), P(("col", "dp"), "row")),
        check_vma=False,
    )
```

time: 2050 us -> 992 us (0.48)
  waiting for transfers between devices: 1840 us -> 287 us
  starting transfers between devices: 0.72 us -> 173 us
  other arithmetic: 59.7 us -> 182 us
  matrix products: 133 us -> 248 us
  local copies, waits for them, and re-layouts: 8.59 us -> 90.6 us
    reduce_scatter x4 -> x0, waiting for transfers between devices: 1380 us -> none  [the longest x1 821 us: shards(): lax.psum_scatter(jnp.concatenate([forward, backward], axis=1), 'row', sca...]
    all_gather x4 -> x0, waiting for transfers between devices: 451 us -> none  [the longest x1 220 us: shards(): lax.all_gather(grad_preact, 'row', axis=0, tiled=True)]
    ppermute x0 -> x83, waiting for transfers between devices: none -> 287 us  [the longest x28 177 us: step(): self.right[t] = lax.ppermute(narrow(right), 'row', up)]
    ppermute x0 -> x83, starting transfers between devices: none -> 173 us  [the longest x28 110 us: step(): self.right[t] = lax.ppermute(narrow(right), 'row', up)]
    convert_element_type x4 -> x29, other arithmetic: 25.5 us -> 128 us  [narrow(): return value.astype(jnp.bfloat16)]
    dot_general x2 -> x18, matrix products: 52.7 us -> 118 us  [contract_last(): lax.dot_general(left, right, (((1,), (1,)), ((), ())), preferred_element_...]
    slice x0 -> x25, local copies, waits for them, and re-layouts: none -> 40.7 us  [the longest x24 38.5 us: replica_sum(): send = lax.slice_in_dim(total, half, 2 * half, axis=axis)]
    concatenate x1 -> x2, other arithmetic: 34.2 us -> 3.31 us  [the longest x1 2.19 us: shards(): jnp.concatenate(out_grads, axis=0)]
  transfers between devices with their start and end apart: 8 -> 83, of which waited for: 8 -> 39; matrix products, arithmetic and copies ran while one was open for 6% -> 45% of each run, Pallas kernels for 0% -> 0%
where the time goes in v1:
time: 992 us; the launch traced here: 984 us
  waiting for transfers between devices  287 us (29%)
  matrix products  248 us (25%)
  other arithmetic  182 us (18%)
  starting transfers between devices  173 us (17%)
  local copies, waits for them, and re-layouts  90.6 us (9%)
    ppermute x28, waiting for transfers between devices, step(): self.right[t] = lax.ppermute(narrow(right), 'row', up)  177 us
    convert_element_type x29, other arithmetic, narrow(): return value.astype(jnp.bfloat16)  128 us
    dot_general x18, matrix products, contract_last(): lax.dot_general(left, right, (((1,), (1,)), ((), ())), preferred_element_...  118 us
    ppermute x28, starting transfers between devices, step(): self.right[t] = lax.ppermute(narrow(right), 'row', up)  110 us
    ppermute x28, waiting for transfers between devices, step(): self.left[t] = lax.ppermute(narrow(left), 'row', down)  82.8 us
    dot_general x12, matrix products, contract_first(): lax.dot_general(left, right, (((0,), (0,)), ((), ())), preferred_element_...  74 us
    dot_general x12, matrix products, ready_forward(): jnp.dot(rows_in, weights[c // halves][0], preferred_element_type=jnp.floa...  56.5 us
    ppermute x28, starting transfers between devices, step(): self.left[t] = lax.ppermute(narrow(left), 'row', down)  40.7 us
  transfers between devices with their start and end apart: 83, of which 39 were waited for; matrix products, arithmetic and copies ran while one was open for 45% of the time, Pallas kernels for 0%

profile of v1, /device:TPU:0, one launch (start us, length us, event | category | flops | bytes accessed | tf_op | source)
XLA Modules:
  0.0 984.2 jit_solution(15443484213230553052)
XLA Ops:
  4.5 7.7 bitcast_convert_fusion.1
  20.7 9.1 constant_dynamic-slice_fusion.7
  45.7 8.1 constant_dynamic-slice_fusion.3
  103.1 6.6 convolution_bitcast_fusion.12
  131.4 11.7 %collective-permute-done.9 = bf16[512,1024]{1,0:T(8,128)(2,1)S(1)} collective-permute-done((bf16[512,1024]{1,0:T(8,128)(2,1)}, bf16[512,1024]{1,0:T(8,128)(2,1)S(1)}, u32[]{:S(2)}, u32[]{:S(2)}) %collective-permute-start.9) | collective-permute-done | bytes 1048608 | tf_op jit(solution)/shard_map/ppermute | solution.py:83
  213.8 11.9 %collective-permute-done.12 = bf16[512,1024]{1,0:T(8,128)(2,1)S(1)} collective-permute-done((bf16[512,1024]{1,0:T(8,128)(2,1)}, bf16[512,1024]{1,0:T(8,128)(2,1)S(1)}, u32[]{:S(2)}, u32[]{:S(2)}) %collective-permute-start.12) | collective-permute-done | bytes 1048608 | tf_op jit(solution)/shard_map/ppermute | solution.py:82
  258.8 6.6 convolution_bitcast_fusion.11
  274.0 10.7 %collective-permute-done.16 = bf16[512,1024]{1,0:T(8,128)(2,1)S(1)} collective-permute-done((bf16[512,1024]{1,0:T(8,128)(2,1)}, bf16[512,1024]{1,0:T(8,128)(2,1)S(1)}, u32[]{:S(2)}, u32[]{:S(2)}) %collective-permute-start.16) | collective-permute-done | bytes 1048608 | tf_op jit(solution)/shard_map/ppermute | solution.py:82
  312.3 8.3 fusion.159
  329.6 7.4 fusion.89
  375.5 6.9 collective-permute-done.22
  386.7 15.6 %collective-permute-done.24 = bf16[512,1024]{1,0:T(8,128)(2,1)S(1)} collective-permute-done((bf16[512,1024]{1,0:T(8,128)(2,1)}, bf16[512,1024]{1,0:T(8,128)(2,1)S(1)}, u32[]{:S(2)}, u32[]{:S(2)}) %collective-permute-start.24) | collective-permute-done | bytes 1048608 | tf_op jit(solution)/shard_map/ppermute | solution.py:82
  418.0 7.9 fusion.157
  425.9 7.6 fusion.156
  460.7 18.1 %collective-permute-done.28 = bf16[512,1024]{1,0:T(8,128)(2,1)S(1)} collective-permute-done((bf16[512,1024]{1,0:T(8,128)(2,1)}, bf16[512,1024]{1,0:T(8,128)(2,1)S(1)}, u32[]{:S(2)}, u32[]{:S(2)}) %collective-permute-start.28) | collective-permute-done | bytes 1048608 | tf_op jit(solution)/shard_map/ppermute | solution.py:82
  523.4 15.7 %collective-permute-done.32 = bf16[512,1024]{1,0:T(8,128)(2,1)S(1)} collective-permute-done((bf16[512,1024]{1,0:T(8,128)(2,1)}, bf16[512,1024]{1,0:T(8,128)(2,1)S(1)}, u32[]{:S(2)}, u32[]{:S(2)}) %collective-permute-start.32) | collective-permute-done | bytes 1048608 | tf_op jit(solution)/shard_map/ppermute | solution.py:82
  553.1 7.6 fusion.155
  560.7 7.5 fusion.154
  577.7 7.4 fusion.97
  599.5 15.0 %collective-permute-done.36 = bf16[512,1024]{1,0:T(8,128)(2,1)S(1)} collective-permute-done((bf16[512,1024]{1,0:T(8,128)(2,1)S(1)}, bf16[512,1024]{1,0:T(8,128)(2,1)S(1)}, u32[]{:S(2)}, u32[]{:S(2)}) %collective-permute-start.36) | collective-permute-done | bytes 1048608 | tf_op jit(solution)/shard_map/ppermute | solution.py:82
  634.7 13.1 %collective-permute-done.40 = bf16[512,1024]{1,0:T(8,128)(2,1)S(1)} collective-permute-done((bf16[512,1024]{1,0:T(8,128)(2,1)S(1)}, bf16[512,1024]{1,0:T(8,128)(2,1)S(1)}, u32[]{:S(2)}, u32[]{:S(2)}) %collective-permute-start.40) | collective-permute-done | bytes 1048608 | tf_op jit(solution)/shard_map/ppermute | solution.py:82
  676.5 12.1 %collective-permute-done.44 = bf16[512,1024]{1,0:T(8,128)(2,1)S(1)} collective-permute-done((bf16[512,1024]{1,0:T(8,128)(2,1)}, bf16[512,1024]{1,0:T(8,128)(2,1)S(1)}, u32[]{:S(2)}, u32[]{:S(2)}) %collective-permute-start.44) | collective-permute-done | bytes 1048608 | tf_op jit(solution)/shard_map/ppermute | solution.py:82
  704.1 10.3 %collective-permute-done.48 = bf16[512,1024]{1,0:T(8,128)(2,1)S(1)} collective-permute-done((bf16[512,1024]{1,0:T(8,128)(2,1)}, bf16[512,1024]{1,0:T(8,128)(2,1)S(1)}, u32[]{:S(2)}, u32[]{:S(2)}) %collective-permute-start.48) | collective-permute-done | bytes 1048608 | tf_op jit(solution)/shard_map/ppermute | solution.py:82
  718.5 8.5 add_convert_fusion
  776.2 10.8 %collective-permute-done.52 = bf16[512,1024]{1,0:T(8,128)(2,1)S(1)} collective-permute-done((bf16[512,1024]{1,0:T(8,128)(2,1)}, bf16[512,1024]{1,0:T(8,128)(2,1)S(1)}, u32[]{:S(2)}, u32[]{:S(2)}) %collective-permute-start.52) | collective-permute-done | bytes 1048608 | tf_op jit(solution)/shard_map/ppermute | solution.py:82
  822.4 7.8 add_convert_fusion.2
  830.2 8.7 fusion.150
  839.0 7.6 fusion.151
  884.6 16.1 %collective-permute-done.54 = bf16[512,1024]{1,0:T(8,128)(2,1)S(1)} collective-permute-done((bf16[512,1024]{1,0:T(8,128)(2,1)}, bf16[512,1024]{1,0:T(8,128)(2,1)S(1)}, u32[]{:S(2)}, u32[]{:S(2)}) %collective-permute-start.54) | collective-permute-done | bytes 1048608 | tf_op jit(solution)/shard_map/ppermute | solution.py:82
  919.1 16.5 %add_add_fusion = f32[1024,1536]{1,0:T(8,128)} fusion(f32[1024,1536]{1,0:T(8,128)} %fusion.151, f32[1024,1536]{1,0:T(8,128)} %fusion.153, f32[1024,1536]{1,0:T(8,128)} %fusion.155, f32[1024,1536]{1,0:T(8,128)} %fusion.159, f32[1024,1536]{1,0:T(8,128)} %fusion.157, bf16[512,1024]{1,0:T(8,128)(2,1)} %copy-done.73, bf16[512,1024]{1,0:T(8,128)(2,1)} %copy-done.72, ...), kind=kOutput, calls=%fused_computation | convolution fusion | flops 3245867008 | bytes 42991616 | tf_op jit(solution)/shard_map/dot_general | solution.py:20
  947.6 27.0 %collective-permute-done.58 = bf16[512,1536]{1,0:T(8,128)(2,1)S(1)} collective-permute-done((bf16[512,1536]{1,0:T(8,128)(2,1)S(1)}, bf16[512,1536]{1,0:T(8,128)(2,1)S(1)}, u32[]{:S(2)}, u32[]{:S(2)}) %collective-permute-start.58) | collective-permute-done | bytes 1572896 | tf_op jit(solution)/shard_map/ppermute | solution.py:189
  977.4 6.6 copy.29
  (728 shorter events, 637.7 us)
Async XLA Ops:
  12.3 107.2 %collective-permute-start = (bf16[512,1024]{1,0:T(8,128)(2,1)}, bf16[512,1024]{1,0:T(8,128)(2,1)S(1)}, u32[]{:S(2)}, u32[]{:S(2)}) collective-permute-start(bf16[512,1024]{1,0:T(8,128)(2,1)} %get-tuple-element.340), channel_id=1, source_target_pairs={{0,2},{2,4},{4,6},{1,3},{3,5},{5,7},{8,10},{10,12},{12,14},{9,11},... | collective-permute-start | bytes 3145736 | tf_op jit(solution)/shard_map/ppermute | solution.py:82
  17.3 102.2 %collective-permute-start.1 = (bf16[512,1024]{1,0:T(8,128)(2,1)}, bf16[512,1024]{1,0:T(8,128)(2,1)}, u32[]{:S(2)}, u32[]{:S(2)}) collective-permute-start(bf16[512,1024]{1,0:T(8,128)(2,1)} %get-tuple-element.340), channel_id=1, source_target_pairs={{2,0},{4,2},{6,4},{3,1},{5,3},{7,5},{10,8},{12,10},{14,12},{11,9},... | collective-permute-start | bytes 3145736 | tf_op jit(solution)/shard_map/ppermute | solution.py:83
  18.6 96.2 %collective-permute-start.2 = (bf16[512,1536]{1,0:T(8,128)(2,1)}, bf16[512,1536]{1,0:T(8,128)(2,1)}, u32[]{:S(2)}, u32[]{:S(2)}) collective-permute-start(bf16[512,1536]{1,0:T(8,128)(2,1)} %param.7), channel_id=1, source_target_pairs={{0,1},{1,0},{2,3},{3,2},{4,5},{5,4},{6,7},{7,6},{8,9},{9,8},{10,11... | collective-permute-start | bytes 4718600 | tf_op jit(solution)/shard_map/ppermute | solution.py:50
  20.1 108.0 %collective-permute-start.5 = (bf16[512,1536]{1,0:T(8,128)(2,1)}, bf16[512,1536]{1,0:T(8,128)(2,1)}, u32[]{:S(2)}, u32[]{:S(2)}) collective-permute-start(bf16[512,1536]{1,0:T(8,128)(2,1)} %param.4), channel_id=1, source_target_pairs={{0,1},{1,0},{2,3},{3,2},{4,5},{5,4},{6,7},{7,6},{8,9},{9,8},{10,11... | collective-permute-start | bytes 4718600 | tf_op jit(solution)/shard_map/ppermute | solution.py:50
  36.1 95.2 %collective-permute-start.8 = (bf16[512,1024]{1,0:T(8,128)(2,1)}, bf16[512,1024]{1,0:T(8,128)(2,1)}, u32[]{:S(2)}, u32[]{:S(2)}) collective-permute-start(bf16[512,1024]{1,0:T(8,128)(2,1)} %get-tuple-element.342), channel_id=1, source_target_pairs={{0,2},{2,4},{4,6},{1,3},{3,5},{5,7},{8,10},{10,12},{12,14},{9,11},... | collective-permute-start | bytes 3145736 | tf_op jit(solution)/shard_map/ppermute | solution.py:82
  122.0 56.4 %collective-permute-start.3 = (bf16[512,1024]{1,0:T(8,128)(2,1)S(1)}, bf16[512,1024]{1,0:T(8,128)(2,1)S(1)}, u32[]{:S(2)}, u32[]{:S(2)}) collective-permute-start(bf16[512,1024]{1,0:T(8,128)(2,1)S(1)} %get-tuple-element.337), channel_id=1, source_target_pairs={{0,2},{2,4},{4,6},{1,3},{3,5},{5,7},{8,10},{10,12},{12,14},{9,11},... | collective-permute-start | bytes 3145736 | tf_op jit(solution)/shard_map/ppermute | solution.py:82
  126.7 51.8 %collective-permute-start.4 = (bf16[512,1024]{1,0:T(8,128)(2,1)S(1)}, bf16[512,1024]{1,0:T(8,128)(2,1)S(1)}, u32[]{:S(2)}, u32[]{:S(2)}) collective-permute-start(bf16[512,1024]{1,0:T(8,128)(2,1)S(1)} %get-tuple-element.336), channel_id=1, source_target_pairs={{2,0},{4,2},{6,4},{3,1},{5,3},{7,5},{10,8},{12,10},{14,12},{11,9},... | collective-permute-start | bytes 3145736 | tf_op jit(solution)/shard_map/ppermute | solution.py:83
  301.2 50.4 %collective-permute-start.18 = (bf16[512,1024]{1,0:T(8,128)(2,1)}, bf16[512,1024]{1,0:T(8,128)(2,1)S(1)}, u32[]{:S(2)}, u32[]{:S(2)}) collective-permute-start(bf16[512,1024]{1,0:T(8,128)(2,1)} %get-tuple-element.281), channel_id=1, source_target_pairs={{0,2},{2,4},{4,6},{1,3},{3,5},{5,7},{8,10},{10,12},{12,14},{9,11},... | collective-permute-start | bytes 3145736 | tf_op jit(solution)/shard_map/ppermute | solution.py:82
  304.9 46.7 %collective-permute-start.19 = (bf16[512,1024]{1,0:T(8,128)(2,1)}, bf16[512,1024]{1,0:T(8,128)(2,1)S(1)}, u32[]{:S(2)}, u32[]{:S(2)}) collective-permute-start(bf16[512,1024]{1,0:T(8,128)(2,1)} %get-tuple-element.280), channel_id=1, source_target_pairs={{2,0},{4,2},{6,4},{3,1},{5,3},{7,5},{10,8},{12,10},{14,12},{11,9},... | collective-permute-start | bytes 3145736 | tf_op jit(solution)/shard_map/ppermute | solution.py:83
  359.8 42.5 %collective-permute-start.24 = (bf16[512,1024]{1,0:T(8,128)(2,1)}, bf16[512,1024]{1,0:T(8,128)(2,1)S(1)}, u32[]{:S(2)}, u32[]{:S(2)}) collective-permute-start(bf16[512,1024]{1,0:T(8,128)(2,1)} %get-tuple-element.283), channel_id=1, source_target_pairs={{0,2},{2,4},{4,6},{1,3},{3,5},{5,7},{8,10},{10,12},{12,14},{9,11},... | collective-permute-start | bytes 3145736 | tf_op jit(solution)/shard_map/ppermute | solution.py:82
  364.5 41.9 %collective-permute-start.25 = (bf16[512,1024]{1,0:T(8,128)(2,1)}, bf16[512,1024]{1,0:T(8,128)(2,1)S(1)}, u32[]{:S(2)}, u32[]{:S(2)}) collective-permute-start(bf16[512,1024]{1,0:T(8,128)(2,1)} %get-tuple-element.282), channel_id=1, source_target_pairs={{2,0},{4,2},{6,4},{3,1},{5,3},{7,5},{10,8},{12,10},{14,12},{11,9},... | collective-permute-start | bytes 3145736 | tf_op jit(solution)/shard_map/ppermute | solution.py:83
  370.0 84.4 %collective-permute-start.60 = (bf16[1536,256]{0,1:T(8,128)(2,1)}, bf16[1536,256]{0,1:T(8,128)(2,1)}, u32[]{:S(2)}, u32[]{:S(2)}) collective-permute-start(bf16[1536,256]{0,1:T(8,128)(2,1)} %slice.399), channel_id=1, source_target_pairs={{0,16},{8,24},{16,0},{24,8},{1,17},{9,25},{17,1},{25,9},{2,18},{10... | collective-permute-start | bytes 2359304 | tf_op jit(solution)/shard_map/ppermute | solution.py:97
  382.4 75.8 %collective-permute-start.72 = (bf16[256,1536]{1,0:T(8,128)(2,1)}, bf16[256,1536]{1,0:T(8,128)(2,1)}, u32[]{:S(2)}, u32[]{:S(2)}) collective-permute-start(bf16[256,1536]{1,0:T(8,128)(2,1)} %slice.393), channel_id=1, source_target_pairs={{0,16},{8,24},{16,0},{24,8},{1,17},{9,25},{17,1},{25,9},{2,18},{10... | collective-permute-start | bytes 2359304 | tf_op jit(solution)/shard_map/ppermute | solution.py:97
  433.5 54.9 %collective-permute-start.26 = (bf16[512,1024]{1,0:T(8,128)(2,1)}, bf16[512,1024]{1,0:T(8,128)(2,1)S(1)}, u32[]{:S(2)}, u32[]{:S(2)}) collective-permute-start(bf16[512,1024]{1,0:T(8,128)(2,1)} %get-tuple-element.273), channel_id=1, source_target_pairs={{0,2},{2,4},{4,6},{1,3},{3,5},{5,7},{8,10},{10,12},{12,14},{9,11},... | collective-permute-start | bytes 3145736 | tf_op jit(solution)/shard_map/ppermute | solution.py:82
  436.0 52.5 %collective-permute-start.27 = (bf16[512,1024]{1,0:T(8,128)(2,1)}, bf16[512,1024]{1,0:T(8,128)(2,1)S(1)}, u32[]{:S(2)}, u32[]{:S(2)}) collective-permute-start(bf16[512,1024]{1,0:T(8,128)(2,1)} %get-tuple-element.272), channel_id=1, source_target_pairs={{2,0},{4,2},{6,4},{3,1},{5,3},{7,5},{10,8},{12,10},{14,12},{11,9},... | collective-permute-start | bytes 3145736 | tf_op jit(solution)/shard_map/ppermute | solution.py:83
  437.3 41.5 %collective-permute-start.28 = (bf16[512,1024]{1,0:T(8,128)(2,1)}, bf16[512,1024]{1,0:T(8,128)(2,1)S(1)}, u32[]{:S(2)}, u32[]{:S(2)}) collective-permute-start(bf16[512,1024]{1,0:T(8,128)(2,1)} %get-tuple-element.279), channel_id=1, source_target_pairs={{0,2},{2,4},{4,6},{1,3},{3,5},{5,7},{8,10},{10,12},{12,14},{9,11},... | collective-permute-start | bytes 3145736 | tf_op jit(solution)/shard_map/ppermute | solution.py:82
  458.2 43.0 %collective-permute-start.61 = (bf16[1536,512]{0,1:T(8,128)(2,1)}, bf16[1536,512]{0,1:T(8,128)(2,1)}, u32[]{:S(2)}, u32[]{:S(2)}) collective-permute-start(bf16[1536,512]{0,1:T(8,128)(2,1)} %slice.385), channel_id=1, source_target_pairs={{0,8},{8,0},{16,24},{24,16},{1,9},{9,1},{17,25},{25,17},{2,10},{10... | collective-permute-start | bytes 4718600 | tf_op jit(solution)/shard_map/ppermute | solution.py:97
  496.5 42.6 %collective-permute-start.32 = (bf16[512,1024]{1,0:T(8,128)(2,1)}, bf16[512,1024]{1,0:T(8,128)(2,1)S(1)}, u32[]{:S(2)}, u32[]{:S(2)}) collective-permute-start(bf16[512,1024]{1,0:T(8,128)(2,1)} %get-tuple-element.275), channel_id=1, source_target_pairs={{0,2},{2,4},{4,6},{1,3},{3,5},{5,7},{8,10},{10,12},{12,14},{9,11},... | collective-permute-start | bytes 3145736 | tf_op jit(solution)/shard_map/ppermute | solution.py:82
  501.2 42.0 %collective-permute-start.33 = (bf16[512,1024]{1,0:T(8,128)(2,1)}, bf16[512,1024]{1,0:T(8,128)(2,1)S(1)}, u32[]{:S(2)}, u32[]{:S(2)}) collective-permute-start(bf16[512,1024]{1,0:T(8,128)(2,1)} %get-tuple-element.274), channel_id=1, source_target_pairs={{2,0},{4,2},{6,4},{3,1},{5,3},{7,5},{10,8},{12,10},{14,12},{11,9},... | collective-permute-start | bytes 3145736 | tf_op jit(solution)/shard_map/ppermute | solution.py:83
  507.6 84.0 %collective-permute-start.62 = (bf16[1536,256]{0,1:T(8,128)(2,1)}, bf16[1536,256]{0,1:T(8,128)(2,1)}, u32[]{:S(2)}, u32[]{:S(2)}) collective-permute-start(bf16[1536,256]{0,1:T(8,128)(2,1)} %slice.398), channel_id=1, source_target_pairs={{0,16},{8,24},{16,0},{24,8},{1,17},{9,25},{17,1},{25,9},{2,18},{10... | collective-permute-start | bytes 2359304 | tf_op jit(solution)/shard_map/ppermute | solution.py:97
  519.1 76.6 %collective-permute-start.74 = (bf16[256,1536]{1,0:T(8,128)(2,1)}, bf16[256,1536]{1,0:T(8,128)(2,1)}, u32[]{:S(2)}, u32[]{:S(2)}) collective-permute-start(bf16[256,1536]{1,0:T(8,128)(2,1)} %slice.392), channel_id=1, source_target_pairs={{0,16},{8,24},{16,0},{24,8},{1,17},{9,25},{17,1},{25,9},{2,18},{10... | collective-permute-start | bytes 2359304 | tf_op jit(solution)/shard_map/ppermute | solution.py:97
  573.1 41.4 %collective-permute-start.36 = (bf16[512,1024]{1,0:T(8,128)(2,1)S(1)}, bf16[512,1024]{1,0:T(8,128)(2,1)S(1)}, u32[]{:S(2)}, u32[]{:S(2)}) collective-permute-start(bf16[512,1024]{1,0:T(8,128)(2,1)S(1)} %copy-done.115), channel_id=1, source_target_pairs={{0,2},{2,4},{4,6},{1,3},{3,5},{5,7},{8,10},{10,12},{12,14},{9,11},... | collective-permute-start | bytes 3145736 | tf_op jit(solution)/shard_map/ppermute | solution.py:82
  595.7 61.2 %collective-permute-start.63 = (bf16[1536,512]{0,1:T(8,128)(2,1)}, bf16[1536,512]{0,1:T(8,128)(2,1)}, u32[]{:S(2)}, u32[]{:S(2)}) collective-permute-start(bf16[1536,512]{0,1:T(8,128)(2,1)} %slice.384), channel_id=1, source_target_pairs={{0,8},{8,0},{16,24},{24,16},{1,9},{9,1},{17,25},{25,17},{2,10},{10... | collective-permute-start | bytes 4718600 | tf_op jit(solution)/shard_map/ppermute | solution.py:97
  598.2 63.9 %collective-permute-start.75 = (bf16[512,1536]{1,0:T(8,128)(2,1)}, bf16[512,1536]{1,0:T(8,128)(2,1)}, u32[]{:S(2)}, u32[]{:S(2)}) collective-permute-start(bf16[512,1536]{1,0:T(8,128)(2,1)} %slice.378), channel_id=1, source_target_pairs={{0,8},{8,0},{16,24},{24,16},{1,9},{9,1},{17,25},{25,17},{2,10},{10... | collective-permute-start | bytes 4718600 | tf_op jit(solution)/shard_map/ppermute | solution.py:97
  754.2 41.8 %collective-permute-start.65 = (bf16[1536,512]{0,1:T(8,128)(2,1)}, bf16[1536,512]{0,1:T(8,128)(2,1)}, u32[]{:S(2)}, u32[]{:S(2)}) collective-permute-start(bf16[1536,512]{0,1:T(8,128)(2,1)} %slice.383), channel_id=1, source_target_pairs={{0,8},{8,0},{16,24},{24,16},{1,9},{9,1},{17,25},{25,17},{2,10},{10... | collective-permute-start | bytes 4718600 | tf_op jit(solution)/shard_map/ppermute | solution.py:97
  796.0 50.7 %collective-permute-start.56 = (bf16[512,1024]{1,0:T(8,128)(2,1)}, bf16[512,1024]{1,0:T(8,128)(2,1)}, u32[]{:S(2)}, u32[]{:S(2)}) collective-permute-start(bf16[512,1024]{1,0:T(8,128)(2,1)} %get-tuple-element.335), channel_id=1, source_target_pairs={{0,2},{2,4},{4,6},{1,3},{3,5},{5,7},{8,10},{10,12},{12,14},{9,11},... | collective-permute-start | bytes 3145736 | tf_op jit(solution)/shard_map/ppermute | solution.py:82
  803.6 43.0 %collective-permute-start.57 = (bf16[512,1024]{1,0:T(8,128)(2,1)}, bf16[512,1024]{1,0:T(8,128)(2,1)}, u32[]{:S(2)}, u32[]{:S(2)}) collective-permute-start(bf16[512,1024]{1,0:T(8,128)(2,1)} %get-tuple-element.334), channel_id=1, source_target_pairs={{2,0},{4,2},{6,4},{3,1},{5,3},{7,5},{10,8},{12,10},{14,12},{11,9},... | collective-permute-start | bytes 3145736 | tf_op jit(solution)/shard_map/ppermute | solution.py:83
  809.4 54.0 %collective-permute-start.66 = (bf16[1536,256]{0,1:T(8,128)(2,1)}, bf16[1536,256]{0,1:T(8,128)(2,1)}, u32[]{:S(2)}, u32[]{:S(2)}) collective-permute-start(bf16[1536,256]{0,1:T(8,128)(2,1)} %slice.396), channel_id=1, source_target_pairs={{0,16},{8,24},{16,0},{24,8},{1,17},{9,25},{17,1},{25,9},{2,18},{10... | collective-permute-start | bytes 2359304 | tf_op jit(solution)/shard_map/ppermute | solution.py:97
  815.1 50.6 %collective-permute-start.78 = (bf16[256,1536]{1,0:T(8,128)(2,1)}, bf16[256,1536]{1,0:T(8,128)(2,1)}, u32[]{:S(2)}, u32[]{:S(2)}) collective-permute-start(bf16[256,1536]{1,0:T(8,128)(2,1)} %slice.390), channel_id=1, source_target_pairs={{0,16},{8,24},{16,0},{24,8},{1,17},{9,25},{17,1},{25,9},{2,18},{10... | collective-permute-start | bytes 2359304 | tf_op jit(solution)/shard_map/ppermute | solution.py:97
  820.8 47.7 %collective-permute-start.80 = (bf16[256,1536]{1,0:T(8,128)(2,1)}, bf16[256,1536]{1,0:T(8,128)(2,1)}, u32[]{:S(2)}, u32[]{:S(2)}) collective-permute-start(bf16[256,1536]{1,0:T(8,128)(2,1)} %slice.389), channel_id=1, source_target_pairs={{0,16},{8,24},{16,0},{24,8},{1,17},{9,25},{17,1},{25,9},{2,18},{10... | collective-permute-start | bytes 2359304 | tf_op jit(solution)/shard_map/ppermute | solution.py:97
  881.1 58.2 %collective-permute-start.68 = (bf16[1536,256]{0,1:T(8,128)(2,1)}, bf16[1536,256]{0,1:T(8,128)(2,1)}, u32[]{:S(2)}, u32[]{:S(2)}) collective-permute-start(bf16[1536,256]{0,1:T(8,128)(2,1)} %slice.395), channel_id=1, source_target_pairs={{0,16},{8,24},{16,0},{24,8},{1,17},{9,25},{17,1},{25,9},{2,18},{10... | collective-permute-start | bytes 2359304 | tf_op jit(solution)/shard_map/ppermute | solution.py:97
  883.0 62.5 %collective-permute-start.82 = (bf16[256,1536]{1,0:T(8,128)(2,1)}, bf16[256,1536]{1,0:T(8,128)(2,1)}, u32[]{:S(2)}, u32[]{:S(2)}) collective-permute-start(bf16[256,1536]{1,0:T(8,128)(2,1)} %slice.388), channel_id=1, source_target_pairs={{0,16},{8,24},{16,0},{24,8},{1,17},{9,25},{17,1},{25,9},{2,18},{10... | collective-permute-start | bytes 2359304 | tf_op jit(solution)/shard_map/ppermute | solution.py:97
  (281 other events, 5036.1 us)

commit v2 on v1

--- a/solution.py
+++ b/solution.py
@@ -48,9 +48,20 @@
         for shift in range(1, n_col):
             pairs = [(i, (i - shift) % n_col) for i in range(n_col)]
             blocks.append(lax.ppermute(block, "col", pairs))
-        return jnp.concatenate(blocks, axis=0)
-
-    tok_all, cot_all = gather(tokens), gather(cotangent)
+        return blocks
+
+    halves = 2
+    group = max(n_col // halves, 1)
+
+    def whole(blocks):
+        return jnp.concatenate(blocks, axis=0) if len(blocks) > 1 else blocks[0]
+
+    def parts_of(blocks):
+        return [whole(blocks[i * group : (i + 1) * group]) for i in range(halves)]
+
+    tok_blocks, cot_blocks = gather(tokens), gather(cotangent)
+    tok_parts, cot_parts = parts_of(tok_blocks), parts_of(cot_blocks)
+    tok_all, cot_all = whole(tok_parts), whole(cot_parts)
 
     slots, bits = [0], []
     bit = n_dp // 2
@@ -71,16 +82,19 @@
             some = next(c for c in cases if c is not None)
             return wide(lax.select_n(row, *[some if c is None else c for c in cases]))
 
-        def step(self, t):
+        def sums(self, t):
             right = self.pick(self.own, t, -1)
             left = self.pick(self.own, t - (n_row - 1), 1)
             if t:
                 right = right + wide(self.right[t - 1])
                 left = left + wide(self.left[t - 1])
+            return narrow(right), narrow(left)
+
+        def send(self, t, right, left):
             up = [(z, z + 1) for z in range(n_row - 1)]
             down = [(z + 1, z) for z in range(n_row - 1)]
-            self.right[t] = lax.ppermute(narrow(right), "row", up)
-            self.left[t] = lax.ppermute(narrow(left), "row", down)
+            self.right[t] = lax.ppermute(right, "row", up)
+            self.left[t] = lax.ppermute(left, "row", down)
 
         def total(self, c):
             right = self.pick({k: v for k, v in self.right.items() if k >= c}, c - 1, 1)
@@ -96,77 +110,72 @@
         pairs = [(i, i ^ bit) for i in range(n_dp)]
         return keep + wide(lax.ppermute(narrow(send), "dp", pairs))
 
-    def replica_sum(total, axis):
+    def replica_sum(product, size, axis):
+        total = None
         for bit in bits:
-            half = total.shape[axis] // 2
-            keep = lax.slice_in_dim(total, 0, half, axis=axis)
-            send = lax.slice_in_dim(total, half, 2 * half, axis=axis)
-            total = exchange(keep, send, bit)
-        return narrow(total)
+            half = size // 2
+            if total is None:
+                keep, send = product(0, half), product(half, size)
+            else:
+                keep = lax.slice_in_dim(total, 0, half, axis=axis)
+                send = lax.slice_in_dim(total, half, size, axis=axis)
+            total, size = exchange(keep, send, bit), half
+        return narrow(product(0, size) if total is None else total)
 
     starts = list(range(0, part, width))
-    halves = 2
     units = len(starts) * halves
-    half = tok_all.shape[0] // halves
     forward, backward = Line(units), Line(units)
     acts, slopes = {}, {}
     in_grads, out_grads, input_total = [], [], None
-    weights = {}
-
-    def load(k):
-        places = [(dp ^ s) * part + starts[k] for s in slots]
-        weights[k] = (
-            jnp.concatenate(
+    w_in, w_out = {}, {}
+
+    def ready_forward(c, place):
+        k, h = c // halves, c % halves
+        if h == 0:
+            places = [(place ^ s) * part + starts[k] for s in slots]
+            w_in[k] = jnp.concatenate(
                 [lax.dynamic_slice_in_dim(weight_in, p, width, axis=1) for p in places], axis=1
-            ),
-            jnp.concatenate(
+            )
+        forward.own[c] = jnp.dot(tok_parts[h], w_in[k], preferred_element_type=jnp.float32)
+
+    def ready_backward(c, place):
+        k, h = c // halves, c % halves
+        if h == 0:
+            places = [(place ^ s) * part + starts[k] for s in slots]
+            w_out[k] = jnp.concatenate(
                 [lax.dynamic_slice_in_dim(weight_out, p, width, axis=0) for p in places], axis=0
-            ),
-        )
-
-    def block(array, h):
-        return array[h * half : (h + 1) * half]
-
-    def ready_forward(c):
-        if c < units:
-            if c // halves not in weights:
-                load(c // halves)
-            rows_in = block(tok_all, c % halves)
-            forward.own[c] = jnp.dot(
-                rows_in, weights[c // halves][0], preferred_element_type=jnp.float32
             )
-
-    def ready_backward(c):
-        if c < units:
-            backward.own[c] = contract_last(block(cot_all, c % halves), weights[c // halves][1])
-
-    def fence(line, t, work):
-        if t:
-            line.right[t - 1], line.left[t - 1], work = lax.optimization_barrier(
-                (line.right[t - 1], line.left[t - 1], work)
-            )
-        return work
-
-    ready_forward(0)
-    ready_backward(0)
+        backward.own[c] = contract_last(cot_parts[h], w_out[k])
+
+    def turn(line, t, place, other_sends):
+        held = (line.own.get(t), line.right.get(t - 1), line.left.get(t - 1))
+        held, place, other_sends = lax.optimization_barrier((held, place, other_sends))
+        for table, key, value in zip(
+            (line.own, line.right, line.left), (t, t - 1, t - 1), held
+        ):
+            if value is not None:
+                table[key] = value
+        return place
+
+    ready_forward(0, dp)
+    ready_backward(0, dp)
+    place, sent = dp, None
     for t in range(forward.steps + 1):
         c = t - (n_row - 1)
-        fresh = forward.own.get(t)
-        fresh = fence(forward, t, fresh)
-        if fresh is not None:
-            forward.own[t] = fresh
+        place = turn(forward, t, place, sent)
+        sent = None
         if t < forward.steps:
-            forward.step(t)
-        ready_forward(t + 1)
-        fresh = backward.own.get(t)
-        fresh = fence(backward, t, (fresh, forward.own.get(t + 1)))
-        if fresh[0] is not None:
-            backward.own[t] = fresh[0]
-        if fresh[1] is not None:
-            forward.own[t + 1] = fresh[1]
+            sent = forward.sums(t)
+            forward.send(t, *sent)
+        if t + 1 < units:
+            ready_forward(t + 1, place)
+        place = turn(backward, t, place, sent)
+        sent = None
         if t < backward.steps:
-            backward.step(t)
-        ready_backward(t + 1)
+            sent = backward.sums(t)
+            backward.send(t, *sent)
+        if t + 1 < units:
+            ready_backward(t + 1, place)
         if c < 0:
             continue
         preact, grad_hidden = forward.total(c), backward.total(c)
@@ -177,9 +186,17 @@
             mine = range(k * halves, (k + 1) * halves)
             activated = jnp.concatenate([acts[i] for i in mine], axis=0)
             grad_preact = jnp.concatenate([slopes[i] for i in mine], axis=0)
-            in_grads.append(replica_sum(contract_first(tok_all, grad_preact), 1))
-            out_grads.append(replica_sum(contract_first(activated, cot_all), 0))
-            term = contract_last(grad_preact, weights[k][0])
+            size = grad_preact.shape[1]
+
+            def in_term(a, b):
+                return contract_first(tok_all, grad_preact[:, a:b])
+
+            def out_term(a, b):
+                return contract_first(activated[:, a:b], cot_all)
+
+            in_grads.append(replica_sum(in_term, size, 1))
+            out_grads.append(replica_sum(out_term, size, 0))
+            term = contract_last(grad_preact, w_in[k])
             input_total = term if input_total is None else input_total + term
 
     input_grad = input_total[:rows]

time: 992 us -> 822 us (0.83)
  waiting for transfers between devices: 287 us -> 147 us
  local copies, waits for them, and re-layouts: 90.6 us -> 63.5 us
  matrix products: 248 us -> 225 us
    ppermute x56, waiting for transfers between devices: 259 us -> 92.6 us  [the longest x28 48.5 us: send(): self.right[t] = lax.ppermute(right, 'row', up)]
    convert_element_type x29 -> x32, other arithmetic: 128 us -> 165 us  [narrow(): return value.astype(jnp.bfloat16)]
    slice x24 -> x12, local copies, waits for them, and re-layouts: 38.5 us -> 8.62 us  [replica_sum(): send = lax.slice_in_dim(total, half, size, axis=axis)]
    add x12 -> x0, other arithmetic: 27.1 us -> none  [exchange(): return keep + wide(lax.ppermute(narrow(send), 'dp', pairs))]
    ppermute x24, waiting for transfers between devices: 0.06 us -> 26.4 us  [exchange(): return keep + wide(lax.ppermute(narrow(send), 'dp', pairs))]
    ppermute x2, waiting for transfers between devices: 0.01 us -> 23.3 us  [gather(): blocks.append(lax.ppermute(block, 'col', pairs))]
    ppermute x1, waiting for transfers between devices: 27 us -> 5.1 us  [shards(): input_grad = input_grad + wide(lax.ppermute(piece, 'col', pairs))]
    dot_general x18, matrix products: 118 us -> 96.4 us  [contract_last(): lax.dot_general(left, right, (((1,), (1,)), ((), ())), preferred_element_...]
  transfers between devices with their start and end apart: 83 -> 83, of which waited for: 39 -> 25; matrix products, arithmetic and copies ran while one was open for 45% -> 58% of each run, Pallas kernels for 0% -> 0%
where the time goes in v2:
time: 822 us; the launch traced here: 812 us
  matrix products  225 us (27%)
  other arithmetic  191 us (23%)
  starting transfers between devices  181 us (22%)
  waiting for transfers between devices  147 us (18%)
  local copies, waits for them, and re-layouts  63.5 us (8%)
    convert_element_type x32, other arithmetic, narrow(): return value.astype(jnp.bfloat16)  165 us
    ppermute x28, starting transfers between devices, send(): self.right[t] = lax.ppermute(right, 'row', up)  121 us
    dot_general x18, matrix products, contract_last(): lax.dot_general(left, right, (((1,), (1,)), ((), ())), preferred_element_...  96.4 us
    dot_general x24, matrix products, contract_first(): lax.dot_general(left, right, (((0,), (0,)), ((), ())), preferred_element_...  90.3 us
    ppermute x28, waiting for transfers between devices, send(): self.right[t] = lax.ppermute(right, 'row', up)  48.5 us
    ppermute x28, waiting for transfers between devices, send(): self.left[t] = lax.ppermute(left, 'row', down)  44.1 us
    dot_general x12, matrix products, ready_forward(): jnp.dot(tok_parts[h], w_in[k], preferred_element_type=jnp.float32)  38.6 us
    ppermute x28, starting transfers between devices, send(): self.left[t] = lax.ppermute(left, 'row', down)  38.5 us
  transfers between devices with their start and end apart: 83, of which 25 were waited for; matrix products, arithmetic and copies ran while one was open for 58% of the time, Pallas kernels for 0%

profile of v2, /device:TPU:0, one launch (start us, length us, event | category | flops | bytes accessed | tf_op | source)
XLA Modules:
  0.0 812.2 jit_solution(16894385838706331992)
XLA Ops:
  33.0 6.2 collective-permute-done.3
  55.0 17.1 %collective-permute-done = bf16[512,1536]{1,0:T(8,128)(2,1)} collective-permute-done((bf16[512,1536]{1,0:T(8,128)(2,1)}, bf16[512,1536]{1,0:T(8,128)(2,1)}, u32[]{:S(2)}, u32[]{:S(2)}) %collective-permute-start) | collective-permute-done | bytes 1572896 | tf_op jit(solution)/shard_map/ppermute | solution.py:50
  130.9 7.0 collective-permute-done.12
  142.5 8.5 %add_convert_fusion.38 = (bf16[512,1024]{0,1:T(8,128)(2,1)}, bf16[512,1024]{0,1:T(8,128)(2,1)}, bf16[512,1024]{0,1:T(8,128)(2,1)}, f32[512,1024]{0,1:T(8,128)}) fusion(bf16[512,1024]{0,1:T(8,128)(2,1)} %collective-permute-done.13, f32[512,1024]{0,1:T(8,128)} %copy-done.34, f32[512,1024]{0,1:T(8,128)} %convolution_bitcast_fusion.16, ...), kind=kLoop, calls=%fused_computation.269 | loop fusion | flops 14680064 | bytes 19922948 | tf_op jit(solution)/shard_map/convert_element_type | solution.py:36
  165.0 8.5 %add_convert_fusion.36 = (bf16[512,1024]{0,1:T(8,128)(2,1)}, bf16[512,1024]{0,1:T(8,128)(2,1)}, bf16[512,1024]{0,1:T(8,128)(2,1)}) fusion(bf16[512,1024]{0,1:T(8,128)(2,1)} %collective-permute-done.11, f32[512,1024]{0,1:T(8,128)} %copy-done.29, f32[512,1024]{0,1:T(8,128)S(1)} %convolution_bitcast_fusion.17, f32[512,1024]{0,1:T(8,128)} %copy-done.36, ...), kind=kLoop, calls=%fused_computation.265 | loop fusion | flops 17301504 | bytes 19922948 | tf_op jit(solution)/shard_map/convert_element_type | solution.py:36
  211.3 6.1 add_convert_fusion.32
  229.7 6.2 fusion.5
  239.4 8.8 %add_convert_fusion.30 = (bf16[512,1024]{0,1:T(8,128)(2,1)}, bf16[512,1024]{0,1:T(8,128)(2,1)}, bf16[512,1024]{0,1:T(8,128)(2,1)}, f32[512,1024]{0,1:T(8,128)}) fusion(bf16[512,1024]{0,1:T(8,128)(2,1)} %collective-permute-done.21, f32[512,1024]{0,1:T(8,128)} %copy-done.24, f32[512,1024]{0,1:T(8,128)} %convolution_bitcast_fusion.12, ...), kind=kLoop, calls=%fused_computation.257 | loop fusion | flops 14680064 | bytes 19922948 | tf_op jit(solution)/shard_map/convert_element_type | solution.py:36
  254.2 8.6 %add_convert_fusion.28 = (bf16[512,1024]{0,1:T(8,128)(2,1)}, bf16[512,1024]{0,1:T(8,128)(2,1)}, bf16[512,1024]{0,1:T(8,128)(2,1)}) fusion(bf16[512,1024]{0,1:T(8,128)(2,1)} %collective-permute-done.19, f32[512,1024]{0,1:T(8,128)} %copy-done.22, f32[512,1024]{0,1:T(8,128)S(1)} %convolution_bitcast_fusion.13, f32[512,1024]{0,1:T(8,128)} %copy-done.29, ...), kind=kLoop, calls=%fused_computation.253 | loop fusion | flops 17301504 | bytes 19922948 | tf_op jit(solution)/shard_map/convert_element_type | solution.py:36
  262.7 6.2 collective-permute-start.22
  283.3 6.3 convolution_bitcast_fusion.9
  317.1 5.9 add_convert_fusion.24
  325.7 6.2 fusion.4
  346.1 7.7 add_convert_fusion.22
  365.2 9.0 %add_convert_fusion.20 = (bf16[512,1024]{0,1:T(8,128)(2,1)}, bf16[512,1024]{0,1:T(8,128)(2,1)}, bf16[512,1024]{0,1:T(8,128)(2,1)}) fusion(bf16[512,1024]{0,1:T(8,128)(2,1)} %collective-permute-done.27, f32[512,1024]{0,1:T(8,128)} %copy-done.16, f32[512,1024]{0,1:T(8,128)} %convolution_bitcast_fusion.9, f32[512,1024]{0,1:T(8,128)} %copy-done.22, ...), kind=kLoop, calls=%fused_computation.241 | loop fusion | flops 17301504 | bytes 19922948 | tf_op jit(solution)/shard_map/convert_element_type | solution.py:36
  392.5 6.3 convolution_bitcast_fusion.5
  434.7 7.5 fusion.3
  455.1 7.8 add_convert_fusion.14
  463.0 6.2 collective-permute-start.40
  473.2 9.2 %add_convert_fusion.12 = (bf16[512,1024]{0,1:T(8,128)(2,1)}, bf16[512,1024]{0,1:T(8,128)(2,1)}, bf16[512,1024]{0,1:T(8,128)(2,1)}) fusion(bf16[512,1024]{0,1:T(8,128)(2,1)} %collective-permute-done.35, f32[512,1024]{0,1:T(8,128)} %copy-done, f32[512,1024]{0,1:T(8,128)} %convolution_bitcast_fusion.5, f32[512,1024]{0,1:T(8,128)} %copy-done.16, ...), kind=kLoop, calls=%fused_computation.229 | loop fusion | flops 17301504 | bytes 19922948 | tf_op jit(solution)/shard_map/convert_element_type | solution.py:36
  539.8 10.1 %collective-permute-done.44 = bf16[512,1024]{0,1:T(8,128)(2,1)S(1)} collective-permute-done((bf16[512,1024]{0,1:T(8,128)(2,1)}, bf16[512,1024]{0,1:T(8,128)(2,1)S(1)}, u32[]{:S(2)}, u32[]{:S(2)}) %collective-permute-start.44) | collective-permute-done | bytes 1048608 | tf_op jit(solution)/shard_map/ppermute | solution.py:96
  563.7 8.7 %collective-permute-done.42 = bf16[512,1024]{0,1:T(8,128)(2,1)S(1)} collective-permute-done((bf16[512,1024]{0,1:T(8,128)(2,1)}, bf16[512,1024]{0,1:T(8,128)(2,1)S(1)}, u32[]{:S(2)}, u32[]{:S(2)}) %collective-permute-start.42) | collective-permute-done | bytes 1048608 | tf_op jit(solution)/shard_map/ppermute | solution.py:96
  582.6 12.3 %collective-permute-done.48 = bf16[512,1024]{0,1:T(8,128)(2,1)} collective-permute-done((bf16[512,1024]{0,1:T(8,128)(2,1)}, bf16[512,1024]{0,1:T(8,128)(2,1)}, u32[]{:S(2)}, u32[]{:S(2)}) %collective-permute-start.48) | collective-permute-done | bytes 1048608 | tf_op jit(solution)/shard_map/ppermute | solution.py:96
  599.3 9.7 %add_convert_fusion.2 = (bf16[512,1024]{0,1:T(8,128)(2,1)}, bf16[512,1024]{0,1:T(8,128)(2,1)}, bf16[512,1024]{0,1:T(8,128)(2,1)}, f32[512,1024]{0,1:T(8,128)S(1)...) fusion(bf16[512,1024]{0,1:T(8,128)(2,1)} %collective-permute-done.4, ...), kind=kLoop, calls=%fused_computation.215 | loop fusion | flops 30932992 | bytes 32505860 | tf_op jit(solution)/shard_map/convert_element_type | solution.py:36
  621.7 6.9 add_convert_fusion
  631.6 6.0 fusion.1
  650.3 8.4 %fusion.2 = f32[1024,1536]{1,0:T(8,128)} fusion(bf16[512,1024]{0,1:T(8,128)(2,1)} %fusion.61, bf16[512,1024]{0,1:T(8,128)(2,1)S(1)} %copy-done.82, bf16[1536,256]{1,0:T(8,128)(2,1)} %copy-done.133, bf16[1536,256]{1,0:T(8,128)(2,1)} %copy-done.134, bf16[1536,256]{1,0:T(8,128)(2,1)} %copy-done.135, bf16[1536,256]{1,0:T(8,128)(2,1)} %copy-done.132), kind=kOutput, calls=%fused_computation.91 | convolution fusion | flops 3238002688 | bytes 11534336 | tf_op jit(solution)/shard_map/dot_general | solution.py:20
  728.0 15.7 %add_add_fusion = f32[1024,1536]{1,0:T(8,128)} fusion(f32[1024,1536]{1,0:T(8,128)} %fusion.1, f32[1024,1536]{1,0:T(8,128)} %fusion.2, f32[1024,1536]{1,0:T(8,128)} %fusion.3, f32[1024,1536]{1,0:T(8,128)} %fusion.5, f32[1024,1536]{1,0:T(8,128)} %fusion.4, bf16[512,1024]{0,1:T(8,128)(2,1)S(1)} %get-tuple-element.352, ...), kind=kOutput, calls=%fused_computation | convolution fusion | flops 3245867008 | bytes 42991616 | tf_op jit(solution)/shard_map/dot_general | solution.py:20
  755.1 13.5 %collective-permute-done.66 = bf16[1536,256]{0,1:T(8,128)(2,1)} collective-permute-done((bf16[1536,256]{0,1:T(8,128)(2,1)}, bf16[1536,256]{0,1:T(8,128)(2,1)}, u32[]{:S(2)}, u32[]{:S(2)}) %collective-permute-start.66) | collective-permute-done | bytes 786464 | tf_op jit(solution)/shard_map/ppermute | solution.py:111
  789.2 6.3 collective-permute-done.70
  796.7 6.6 copy.13
  803.3 6.5 collective-permute-done.82
  (629 shorter events, 542.2 us)
Async XLA Ops:
  14.0 58.1 %collective-permute-start = (bf16[512,1536]{1,0:T(8,128)(2,1)}, bf16[512,1536]{1,0:T(8,128)(2,1)}, u32[]{:S(2)}, u32[]{:S(2)}) collective-permute-start(bf16[512,1536]{1,0:T(8,128)(2,1)} %param.7), channel_id=1, source_target_pairs={{0,1},{1,0},{2,3},{3,2},{4,5},{5,4},{6,7},{7,6},{8,9},{9,8},{10,11... | collective-permute-start | bytes 4718600 | tf_op jit(solution)/shard_map/ppermute | solution.py:50
  23.5 51.8 %collective-permute-start.1 = (bf16[512,1024]{0,1:T(8,128)(2,1)}, bf16[512,1024]{0,1:T(8,128)(2,1)}, u32[]{:S(2)}, u32[]{:S(2)}) collective-permute-start(bf16[512,1024]{0,1:T(8,128)(2,1)} %convert_element_type.700), channel_id=1, source_target_pairs={{0,2},{2,4},{4,6},{1,3},{3,5},{5,7},{8,10},{10,12},{12,14},{9,11},... | collective-permute-start | bytes 3145736 | tf_op jit(solution)/shard_map/ppermute | solution.py:96
  48.9 57.4 %collective-permute-start.8 = (bf16[512,1024]{0,1:T(8,128)(2,1)}, bf16[512,1024]{0,1:T(8,128)(2,1)S(1)}, u32[]{:S(2)}, u32[]{:S(2)}) collective-permute-start(bf16[512,1024]{0,1:T(8,128)(2,1)} %get-tuple-element.362), channel_id=1, source_target_pairs={{0,2},{2,4},{4,6},{1,3},{3,5},{5,7},{8,10},{10,12},{12,14},{9,11},... | collective-permute-start | bytes 3145736 | tf_op jit(solution)/shard_map/ppermute | solution.py:96
  53.7 52.7 %collective-permute-start.9 = (bf16[512,1024]{0,1:T(8,128)(2,1)}, bf16[512,1024]{0,1:T(8,128)(2,1)}, u32[]{:S(2)}, u32[]{:S(2)}) collective-permute-start(bf16[512,1024]{0,1:T(8,128)(2,1)} %get-tuple-element.361), channel_id=1, source_target_pairs={{2,0},{4,2},{6,4},{3,1},{5,3},{7,5},{10,8},{12,10},{14,12},{11,9},... | collective-permute-start | bytes 3145736 | tf_op jit(solution)/shard_map/ppermute | solution.py:97
  151.1 47.7 %collective-permute-start.16 = (bf16[512,1024]{0,1:T(8,128)(2,1)}, bf16[512,1024]{0,1:T(8,128)(2,1)S(1)}, u32[]{:S(2)}, u32[]{:S(2)}) collective-permute-start(bf16[512,1024]{0,1:T(8,128)(2,1)} %get-tuple-element.313), channel_id=1, source_target_pairs={{0,2},{2,4},{4,6},{1,3},{3,5},{5,7},{8,10},{10,12},{12,14},{9,11},... | collective-permute-start | bytes 3145736 | tf_op jit(solution)/shard_map/ppermute | solution.py:96
  154.5 44.4 %collective-permute-start.17 = (bf16[512,1024]{0,1:T(8,128)(2,1)}, bf16[512,1024]{0,1:T(8,128)(2,1)}, u32[]{:S(2)}, u32[]{:S(2)}) collective-permute-start(bf16[512,1024]{0,1:T(8,128)(2,1)} %get-tuple-element.312), channel_id=1, source_target_pairs={{2,0},{4,2},{6,4},{3,1},{5,3},{7,5},{10,8},{12,10},{14,12},{11,9},... | collective-permute-start | bytes 3145736 | tf_op jit(solution)/shard_map/ppermute | solution.py:97
  229.7 60.0 %collective-permute-start.71 = (bf16[512,1536]{1,0:T(8,128)(2,1)}, bf16[512,1536]{1,0:T(8,128)(2,1)}, u32[]{:S(2)}, u32[]{:S(2)}) collective-permute-start(bf16[512,1536]{1,0:T(8,128)(2,1)} %convolution_convert_fusion.11), channel_id=1, source_target_pairs={{0,8},{8,0},{16,24},{24,16},{1,9},{9,1},{17,25},{25,17},{2,10},{10... | collective-permute-start | bytes 4718600 | tf_op jit(solution)/shard_map/ppermute | solution.py:111
  238.9 56.7 %collective-permute-start.59 = (bf16[1536,512]{0,1:T(8,128)(2,1)}, bf16[1536,512]{0,1:T(8,128)(2,1)}, u32[]{:S(2)}, u32[]{:S(2)}) collective-permute-start(bf16[1536,512]{0,1:T(8,128)(2,1)} %convolution_convert_fusion.5), channel_id=1, source_target_pairs={{0,8},{8,0},{16,24},{24,16},{1,9},{9,1},{17,25},{25,17},{2,10},{10... | collective-permute-start | bytes 4718600 | tf_op jit(solution)/shard_map/ppermute | solution.py:111
  248.2 53.4 %collective-permute-start.24 = (bf16[512,1024]{0,1:T(8,128)(2,1)}, bf16[512,1024]{0,1:T(8,128)(2,1)S(1)}, u32[]{:S(2)}, u32[]{:S(2)}) collective-permute-start(bf16[512,1024]{0,1:T(8,128)(2,1)} %get-tuple-element.305), channel_id=1, source_target_pairs={{0,2},{2,4},{4,6},{1,3},{3,5},{5,7},{8,10},{10,12},{12,14},{9,11},... | collective-permute-start | bytes 3145736 | tf_op jit(solution)/shard_map/ppermute | solution.py:96
  252.8 49.3 %collective-permute-start.25 = (bf16[512,1024]{0,1:T(8,128)(2,1)}, bf16[512,1024]{0,1:T(8,128)(2,1)}, u32[]{:S(2)}, u32[]{:S(2)}) collective-permute-start(bf16[512,1024]{0,1:T(8,128)(2,1)} %get-tuple-element.304), channel_id=1, source_target_pairs={{2,0},{4,2},{6,4},{3,1},{5,3},{7,5},{10,8},{12,10},{14,12},{11,9},... | collective-permute-start | bytes 3145736 | tf_op jit(solution)/shard_map/ppermute | solution.py:97
  262.7 49.7 %collective-permute-start.22 = (bf16[512,1024]{0,1:T(8,128)(2,1)}, bf16[512,1024]{0,1:T(8,128)(2,1)}, u32[]{:S(2)}, u32[]{:S(2)}) collective-permute-start(bf16[512,1024]{0,1:T(8,128)(2,1)} %get-tuple-element.303), channel_id=1, source_target_pairs={{0,2},{2,4},{4,6},{1,3},{3,5},{5,7},{8,10},{10,12},{12,14},{9,11},... | collective-permute-start | bytes 3145736 | tf_op jit(solution)/shard_map/ppermute | solution.py:96
  295.6 44.2 %collective-permute-start.72 = (bf16[256,1536]{1,0:T(8,128)(2,1)S(1)}, bf16[256,1536]{1,0:T(8,128)(2,1)}, u32[]{:S(2)}, u32[]{:S(2)}) collective-permute-start(bf16[256,1536]{1,0:T(8,128)(2,1)S(1)} %slice.501), channel_id=1, source_target_pairs={{0,16},{8,24},{16,0},{24,8},{1,17},{9,25},{17,1},{25,9},{2,18},{10... | collective-permute-start | bytes 2359304 | tf_op jit(solution)/shard_map/ppermute | solution.py:111
  343.3 55.5 %collective-permute-start.73 = (bf16[512,1536]{1,0:T(8,128)(2,1)}, bf16[512,1536]{1,0:T(8,128)(2,1)}, u32[]{:S(2)}, u32[]{:S(2)}) collective-permute-start(bf16[512,1536]{1,0:T(8,128)(2,1)} %convolution_convert_fusion.10), channel_id=1, source_target_pairs={{0,8},{8,0},{16,24},{24,16},{1,9},{9,1},{17,25},{25,17},{2,10},{10... | collective-permute-start | bytes 4718600 | tf_op jit(solution)/shard_map/ppermute | solution.py:111
  345.6 59.1 %collective-permute-start.61 = (bf16[1536,512]{0,1:T(8,128)(2,1)}, bf16[1536,512]{0,1:T(8,128)(2,1)}, u32[]{:S(2)}, u32[]{:S(2)}) collective-permute-start(bf16[1536,512]{0,1:T(8,128)(2,1)} %convolution_convert_fusion.4), channel_id=1, source_target_pairs={{0,8},{8,0},{16,24},{24,16},{1,9},{9,1},{17,25},{25,17},{2,10},{10... | collective-permute-start | bytes 4718600 | tf_op jit(solution)/shard_map/ppermute | solution.py:111
  353.8 56.0 %collective-permute-start.32 = (bf16[512,1024]{0,1:T(8,128)(2,1)}, bf16[512,1024]{0,1:T(8,128)(2,1)}, u32[]{:S(2)}, u32[]{:S(2)}) collective-permute-start(bf16[512,1024]{0,1:T(8,128)(2,1)} %get-tuple-element.297), channel_id=1, source_target_pairs={{0,2},{2,4},{4,6},{1,3},{3,5},{5,7},{8,10},{10,12},{12,14},{9,11},... | collective-permute-start | bytes 3145736 | tf_op jit(solution)/shard_map/ppermute | solution.py:96
  359.4 51.0 %collective-permute-start.33 = (bf16[512,1024]{0,1:T(8,128)(2,1)}, bf16[512,1024]{0,1:T(8,128)(2,1)}, u32[]{:S(2)}, u32[]{:S(2)}) collective-permute-start(bf16[512,1024]{0,1:T(8,128)(2,1)} %get-tuple-element.296), channel_id=1, source_target_pairs={{2,0},{4,2},{6,4},{3,1},{5,3},{7,5},{10,8},{12,10},{14,12},{11,9},... | collective-permute-start | bytes 3145736 | tf_op jit(solution)/shard_map/ppermute | solution.py:97
  374.3 47.2 %collective-permute-start.30 = (bf16[512,1024]{0,1:T(8,128)(2,1)}, bf16[512,1024]{0,1:T(8,128)(2,1)S(1)}, u32[]{:S(2)}, u32[]{:S(2)}) collective-permute-start(bf16[512,1024]{0,1:T(8,128)(2,1)} %get-tuple-element.295), channel_id=1, source_target_pairs={{0,2},{2,4},{4,6},{1,3},{3,5},{5,7},{8,10},{10,12},{12,14},{9,11},... | collective-permute-start | bytes 3145736 | tf_op jit(solution)/shard_map/ppermute | solution.py:96
  404.7 45.3 %collective-permute-start.74 = (bf16[256,1536]{1,0:T(8,128)(2,1)S(1)}, bf16[256,1536]{1,0:T(8,128)(2,1)S(1)}, u32[]{:S(2)}, u32[]{:S(2)}) collective-permute-start(bf16[256,1536]{1,0:T(8,128)(2,1)S(1)} %slice.500), channel_id=1, source_target_pairs={{0,16},{8,24},{16,0},{24,8},{1,17},{9,25},{17,1},{25,9},{2,18},{10... | collective-permute-start | bytes 2359304 | tf_op jit(solution)/shard_map/ppermute | solution.py:111
  409.8 42.6 %collective-permute-start.62 = (bf16[1536,256]{0,1:T(8,128)(2,1)S(1)}, bf16[1536,256]{0,1:T(8,128)(2,1)}, u32[]{:S(2)}, u32[]{:S(2)}) collective-permute-start(bf16[1536,256]{0,1:T(8,128)(2,1)S(1)} %slice.506), channel_id=1, source_target_pairs={{0,16},{8,24},{16,0},{24,8},{1,17},{9,25},{17,1},{25,9},{2,18},{10... | collective-permute-start | bytes 2359304 | tf_op jit(solution)/shard_map/ppermute | solution.py:111
  452.4 49.5 %collective-permute-start.75 = (bf16[512,1536]{1,0:T(8,128)(2,1)}, bf16[512,1536]{1,0:T(8,128)(2,1)}, u32[]{:S(2)}, u32[]{:S(2)}) collective-permute-start(bf16[512,1536]{1,0:T(8,128)(2,1)} %convolution_convert_fusion.9), channel_id=1, source_target_pairs={{0,8},{8,0},{16,24},{24,16},{1,9},{9,1},{17,25},{25,17},{2,10},{10... | collective-permute-start | bytes 4718600 | tf_op jit(solution)/shard_map/ppermute | solution.py:111
  454.6 54.2 %collective-permute-start.63 = (bf16[1536,512]{0,1:T(8,128)(2,1)}, bf16[1536,512]{0,1:T(8,128)(2,1)}, u32[]{:S(2)}, u32[]{:S(2)}) collective-permute-start(bf16[1536,512]{0,1:T(8,128)(2,1)} %convolution_convert_fusion.3), channel_id=1, source_target_pairs={{0,8},{8,0},{16,24},{24,16},{1,9},{9,1},{17,25},{25,17},{2,10},{10... | collective-permute-start | bytes 4718600 | tf_op jit(solution)/shard_map/ppermute | solution.py:111
  463.0 53.8 %collective-permute-start.40 = (bf16[512,1024]{0,1:T(8,128)(2,1)}, bf16[512,1024]{0,1:T(8,128)(2,1)}, u32[]{:S(2)}, u32[]{:S(2)}) collective-permute-start(bf16[512,1024]{0,1:T(8,128)(2,1)} %get-tuple-element.289), channel_id=1, source_target_pairs={{0,2},{2,4},{4,6},{1,3},{3,5},{5,7},{8,10},{10,12},{12,14},{9,11},... | collective-permute-start | bytes 3145736 | tf_op jit(solution)/shard_map/ppermute | solution.py:96
  469.2 47.8 %collective-permute-start.41 = (bf16[512,1024]{0,1:T(8,128)(2,1)}, bf16[512,1024]{0,1:T(8,128)(2,1)}, u32[]{:S(2)}, u32[]{:S(2)}) collective-permute-start(bf16[512,1024]{0,1:T(8,128)(2,1)} %get-tuple-element.288), channel_id=1, source_target_pairs={{2,0},{4,2},{6,4},{3,1},{5,3},{7,5},{10,8},{12,10},{14,12},{11,9},... | collective-permute-start | bytes 3145736 | tf_op jit(solution)/shard_map/ppermute | solution.py:97
  482.4 43.7 %collective-permute-start.38 = (bf16[512,1024]{0,1:T(8,128)(2,1)}, bf16[512,1024]{0,1:T(8,128)(2,1)}, u32[]{:S(2)}, u32[]{:S(2)}) collective-permute-start(bf16[512,1024]{0,1:T(8,128)(2,1)} %get-tuple-element.287), channel_id=1, source_target_pairs={{0,2},{2,4},{4,6},{1,3},{3,5},{5,7},{8,10},{10,12},{12,14},{9,11},... | collective-permute-start | bytes 3145736 | tf_op jit(solution)/shard_map/ppermute | solution.py:96
  516.8 44.2 %collective-permute-start.64 = (bf16[1536,256]{0,1:T(8,128)(2,1)}, bf16[1536,256]{0,1:T(8,128)(2,1)}, u32[]{:S(2)}, u32[]{:S(2)}) collective-permute-start(bf16[1536,256]{0,1:T(8,128)(2,1)} %slice.505), channel_id=1, source_target_pairs={{0,16},{8,24},{16,0},{24,8},{1,17},{9,25},{17,1},{25,9},{2,18},{10... | collective-permute-start | bytes 2359304 | tf_op jit(solution)/shard_map/ppermute | solution.py:111
  609.1 54.7 %collective-permute-start.52 = (bf16[512,1024]{0,1:T(8,128)(2,1)}, bf16[512,1024]{0,1:T(8,128)(2,1)S(1)}, u32[]{:S(2)}, u32[]{:S(2)}) collective-permute-start(bf16[512,1024]{0,1:T(8,128)(2,1)} %get-tuple-element.317), channel_id=1, source_target_pairs={{0,2},{2,4},{4,6},{1,3},{3,5},{5,7},{8,10},{10,12},{12,14},{9,11},... | collective-permute-start | bytes 3145736 | tf_op jit(solution)/shard_map/ppermute | solution.py:96
  611.0 56.3 %collective-permute-start.53 = (bf16[512,1024]{0,1:T(8,128)(2,1)}, bf16[512,1024]{0,1:T(8,128)(2,1)S(1)}, u32[]{:S(2)}, u32[]{:S(2)}) collective-permute-start(bf16[512,1024]{0,1:T(8,128)(2,1)} %get-tuple-element.316), channel_id=1, source_target_pairs={{2,0},{4,2},{6,4},{3,1},{5,3},{7,5},{10,8},{12,10},{14,12},{11,9},... | collective-permute-start | bytes 3145736 | tf_op jit(solution)/shard_map/ppermute | solution.py:97
  699.1 52.3 %collective-permute-start.80 = (bf16[256,1536]{1,0:T(8,128)(2,1)}, bf16[256,1536]{1,0:T(8,128)(2,1)}, u32[]{:S(2)}, u32[]{:S(2)}) collective-permute-start(bf16[256,1536]{1,0:T(8,128)(2,1)} %slice.497), channel_id=1, source_target_pairs={{0,16},{8,24},{16,0},{24,8},{1,17},{9,25},{17,1},{25,9},{2,18},{10... | collective-permute-start | bytes 2359304 | tf_op jit(solution)/shard_map/ppermute | solution.py:111
  705.1 43.2 %collective-permute-start.78 = (bf16[256,1536]{1,0:T(8,128)(2,1)}, bf16[256,1536]{1,0:T(8,128)(2,1)}, u32[]{:S(2)}, u32[]{:S(2)}) collective-permute-start(bf16[256,1536]{1,0:T(8,128)(2,1)} %slice.498), channel_id=1, source_target_pairs={{0,16},{8,24},{16,0},{24,8},{1,17},{9,25},{17,1},{25,9},{2,18},{10... | collective-permute-start | bytes 2359304 | tf_op jit(solution)/shard_map/ppermute | solution.py:111
  707.3 63.6 %collective-permute-start.68 = (bf16[1536,256]{0,1:T(8,128)(2,1)}, bf16[1536,256]{0,1:T(8,128)(2,1)}, u32[]{:S(2)}, u32[]{:S(2)}) collective-permute-start(bf16[1536,256]{0,1:T(8,128)(2,1)} %slice.503), channel_id=1, source_target_pairs={{0,16},{8,24},{16,0},{24,8},{1,17},{9,25},{17,1},{25,9},{2,18},{10... | collective-permute-start | bytes 2359304 | tf_op jit(solution)/shard_map/ppermute | solution.py:111
  718.5 50.0 %collective-permute-start.66 = (bf16[1536,256]{0,1:T(8,128)(2,1)}, bf16[1536,256]{0,1:T(8,128)(2,1)}, u32[]{:S(2)}, u32[]{:S(2)}) collective-permute-start(bf16[1536,256]{0,1:T(8,128)(2,1)} %slice.504), channel_id=1, source_target_pairs={{0,16},{8,24},{16,0},{24,8},{1,17},{9,25},{17,1},{25,9},{2,18},{10... | collective-permute-start | bytes 2359304 | tf_op jit(solution)/shard_map/ppermute | solution.py:111
  724.4 52.4 %collective-permute-start.81 = (bf16[512,1536]{1,0:T(8,128)(2,1)}, bf16[512,1536]{1,0:T(8,128)(2,1)}, u32[]{:S(2)}, u32[]{:S(2)}) collective-permute-start(bf16[512,1536]{1,0:T(8,128)(2,1)} %convolution_convert_fusion.6), channel_id=1, source_target_pairs={{0,8},{8,0},{16,24},{24,16},{1,9},{9,1},{17,25},{25,17},{2,10},{10... | collective-permute-start | bytes 4718600 | tf_op jit(solution)/shard_map/ppermute | solution.py:111
  (234 other events, 3419.6 us)
